TPU v7x, 32 devices: a whole 2x2x4 slice. The times are simulated.
32 devices in a mesh: grp: 2 (over y), step: 4 (over z), chain: 2 (over x), rep: 2 (over core).
Axes of the slice: x: 2, y: 2, z: 4, core: 2. Of those that a mesh axis runs over, the one named last changes fastest.
Arguments:
- init_seed: int32 [8], P(('grp', 'chain', 'rep')), parts along dimension 0, may hold values from 0 to 63
- noise_index: int32 [8, 32], P(('grp', 'chain', 'rep'), 'step'), parts along dimension 0, may hold values from 0 to 4095
- init_table: float32 [64, 256], replicated, may hold values from -6 to 6
- noise_table: float32 [4096, 256], replicated, may hold values from -6 to 6
- weight: float32 [256, 256], replicated
- bias: float32 [256], replicated, may hold values from -3 to 3
- rates: float32 [64, 256], P(('grp', 'step')), parts along dimension 0, may hold values from 0 to 0.5
- old_path: float32 [8, 32, 256], P(('grp', 'chain', 'rep'), 'step'), parts along dimension 0, may hold values from -6 to 6
- cotangent: float32 [8, 32, 256], P(('grp', 'chain', 'rep'), 'step'), parts along dimension 0, may hold values from -0.3 to 0.3
Outputs:
- path_new: float32 [8, 32, 256], P(('grp', 'chain', 'rep'), 'step'), parts along dimension 0
- grad_w: float32 [512, 256], P('grp'), parts along dimension 0
- grad_b: float32 [512], P('grp'), parts along dimension 0
There are 2 independent parts, one for each index of `grp`. A program takes and returns all parts, laid end to end along the dimension named above; an argument that names none is the same for every part. Nothing has to cross between parts.
All inputs are finite; a program needn't handle non-finite values.
Results may differ from a plain program's by a relative error of at most 0.0001.
Values sent between devices are 32-bit elements; how exact they have to be, the bound alone decides.
A program may use at most 64 MiB of HBM per device.

v0:
```python
import jax
import jax.numpy as jnp
from jax import lax
from jax.sharding import PartitionSpec as P


def shifted_2(block, axis, distance):
    devices = range(lax.axis_size(axis))
    route = [(i - distance, i) for i in devices if i - distance in devices]
    return lax.ppermute(block, axis, route)


def carried_in(x, axis, combine, identity, reverse):
    length, mine = (lax.axis_size(axis), lax.axis_index(axis))
    everything = jax.tree.map(lambda part: lax.all_gather(part, axis), x)
    start = jax.tree.map(
        lambda part, zero: jnp.broadcast_to(jnp.asarray(zero, part.dtype), part.shape), x, identity
    )

    def turn(k, before):
        at = length - 1 - k if reverse else k
        reached = at > mine if reverse else at < mine
        new = combine(before, jax.tree.map(lambda part: part[at], everything))
        return jax.tree.map(lambda a, b: jnp.where(reached, a, b), new, before)

    return lax.fori_loop(0, length, turn, start)


def compose(earlier, later):
    early_mat, early_vec = earlier
    late_mat, late_vec = later
    highest = lax.Precision.HIGHEST
    new_mat = jnp.einsum("...ij,...jk->...ik", late_mat, early_mat, precision=highest)
    new_vec = jnp.einsum("...ij,...j->...i", late_mat, early_vec, precision=highest) + late_vec
    return (new_mat, new_vec)


def shards(
    init_seed, noise_index, init_table, noise_table, weight, bias, rates, old_path, cotangent
):
    highest = lax.Precision.HIGHEST
    chains, steps, width = old_path.shape
    ranks = lax.axis_size("step")
    position = lax.axis_index("step")
    step_size = 4.0 / (steps * ranks)
    start_state = init_table[init_seed]
    shifted = shifted_2(old_path[:, -1], "step", 1)
    first_prev = jnp.where(position == 0, start_state, shifted)
    previous = jnp.concatenate([first_prev[:, None], old_path[:, :-1]], axis=1)
    mixed = jnp.einsum("ctj,ij->cti", previous, weight, precision=highest)
    squash = jnp.tanh(mixed + bias + noise_table[noise_index])
    slope = 1.0 - squash * squash
    keep_rate = 1.0 - rates
    offset = step_size * (squash - slope * mixed)
    identity = jnp.eye(width, dtype=jnp.float32)
    jacobian = keep_rate[None, :, :, None] * identity + step_size * slope[:, :, :, None] * weight
    prefix_mat, prefix_vec = lax.associative_scan(compose, (jacobian, offset), axis=1)
    transposed = jnp.swapaxes(jacobian, 2, 3)
    source = jnp.einsum("ctij,ctj->cti", transposed, cotangent, precision=highest)
    flip_mat, flip_vec = lax.associative_scan(
        compose, (jnp.flip(transposed, 1), jnp.flip(source, 1)), axis=1
    )
    suffix_mat = jnp.flip(flip_mat, 1)
    suffix_vec = jnp.flip(flip_vec, 1)
    block_mat = prefix_mat[:, -1]
    block_vec = prefix_vec[:, -1]
    back_vec = suffix_vec[:, 0]
    neutral = (jnp.broadcast_to(identity, block_mat.shape), jnp.zeros_like(block_vec))
    ahead_mat, ahead_vec = carried_in((block_mat, block_vec), "step", compose, neutral, False)
    entry_state = jnp.einsum("cij,cj->ci", ahead_mat, start_state, precision=highest) + ahead_vec
    behind_mat, adjoint_in = carried_in(
        (suffix_mat[:, 0], back_vec), "step", compose, neutral, True
    )
    path_new = jnp.einsum("ctij,cj->cti", prefix_mat, entry_state, precision=highest) + prefix_vec
    carried = jnp.einsum("ctij,cj->cti", suffix_mat, adjoint_in, precision=highest) + suffix_vec
    following = jnp.concatenate([carried[:, 1:], adjoint_in[:, None]], axis=1)
    adjoint = cotangent + following
    weighted = adjoint * slope
    grad_local = step_size * jnp.einsum("cti,ctj->ij", weighted, previous, precision=highest)
    bias_local = step_size * jnp.sum(weighted, axis=(0, 1))
    grad_w, grad_b = lax.psum((grad_local, bias_local), ("step", "chain", "rep"))
    return (path_new, grad_w, grad_b)


def solution(mesh):
    placed = (
        P(("grp", "chain", "rep")),
        P(("grp", "chain", "rep"), "step"),
        P(),
        P(),
        P(),
        P(),
        P(("grp", "step"), None),
        P(("grp", "chain", "rep"), "step", None),
        P(("grp", "chain", "rep"), "step", None),
    )
    return jax.shard_map(
        shards,
        mesh=mesh,
        in_specs=placed,
        out_specs=(P(("grp", "chain", "rep"), "step", None), P("grp", None), P("grp")),
        check_vma=False,
    )
```

profile of v0, /device:TPU:1, one launch (start us, length us, event | category | flops | bytes accessed | tf_op | source)
XLA Modules:
  0.0 272.3 jit_solution(16754340663512875002)
XLA Ops:
  7.2 0.7 slice_bitcast_fusion.12
  8.0 4.0 %collective-permute-start = (f32[1,256]{1,0:T(1,128)S(1)}, f32[1,256]{1,0:T(1,128)S(1)}, u32[]{:S(2)}, u32[]{:S(2)}) collective-permute-start(f32[1,256]{1,0:T(1,128)S(1)} %slice_bitcast_fusion.12), channel_id=1, source_target_pairs={{0,4},{4,8},{8,12},{1,5},{5,9},{9,13},{2,6},{6,10},{10,14},{3,7},{... | collective-permute-start | bytes 3080 | tf_op jit(solution)/shard_map/ppermute | solution.py:10
  13.4 2.8 %gather_fusion = f32[8,256]{1,0:T(8,128)S(1)} fusion(f32[4096,256]{1,0:T(8,128)} %param.16, s32[1024]{0:T(1024)S(1)} %pad_clamp_fusion), kind=kCustom, calls=%fused_computation | custom fusion | bytes 16416 | tf_op jit(solution)/shard_map/gather | solution.py:51
  16.8 1.2 fusion.88
  18.1 0.8 multiply_bitcast_fusion
  18.9 2.4 fusion.21
  21.5 1.7 fusion.83
  23.2 1.0 fusion.36
  24.2 0.7 slice.260
  25.0 2.1 slice.222
  27.1 1.5 fusion.121
  28.5 1.3 slice.225
  30.6 1.1 convolution_bitcast_fusion.2
  34.5 0.9 pad_add_fusion.1
  35.3 0.8 pad_maximum_fusion.2
  36.1 1.1 pad.78
  37.3 2.8 %pad.79 = f32[1,4,256,256]{3,2,1,0:T(8,128)} pad(f32[1,2,256,256]{3,2,1,0:T(8,128)} %pad_add_fusion.1, f32[]{:T(128)} %constant.88.clone.1), padding=0_0_0x1_0_1x0_0_0x0_0_0 | pad | bytes 1572868 | tf_op jit(solution)/shard_map/pad | solution.py:57
  40.1 3.1 %convolution_bitcast_fusion.4 = f32[1,3,256,256]{3,2,1,0:T(8,128)} fusion(f32[1,4,256,256]{3,2,1,0:T(8,128)} %pad.79, f32[1,4,256,256]{3,2,1,0:T(8,128)S(1)} %pad.78, f32[1,8,256,256]{3,2,1,0:T(8,128)S(1)} %get-tuple-element.325), kind=kOutput, calls=%fused_computation.38 | convolution fusion | flops 604176384 | bytes 3145728 | tf_op jit(solution)/shard_map/...ij,...jk->...ik/dot_general | solution.py:33
  43.2 1.1 add.246
  44.3 2.3 slice.227
  46.6 3.4 %convolution_bitcast_fusion.1 = f32[1,4,256,256]{3,2,1,0:T(8,128)S(1)} fusion(f32[1,4,256,256]{2,3,1,0:T(8,128)} %slice.227, f32[1,4,256,256]{2,3,1,0:T(8,128)} %copy-done.3), kind=kOutput, calls=%fused_computation.35 | convolution fusion | flops 805306368 | bytes 3145728 | tf_op jit(solution)/shard_map/...ij,...jk->...ik/dot_general | solution.py:33
  52.2 2.1 slice.223
  54.3 0.7 fusion.53
  55.1 2.3 pad_maximum_fusion
  57.4 2.2 pad.80
  59.6 4.7 %pad.81 = f32[1,8,256,256]{3,2,1,0:T(8,128)} pad(f32[1,4,256,256]{3,2,1,0:T(8,128)} %add.246, f32[]{:T(128)} %constant.88.clone.1), padding=0_0_0x1_0_1x0_0_0x0_0_0 | pad | bytes 3145732 | tf_op jit(solution)/shard_map/pad | solution.py:57
  64.3 1.7 slice_add_fusion.1
  66.2 1.7 fusion.50
  67.9 1.0 slice.282
  69.0 0.8 copy.19
  71.0 0.8 pad_add_fusion
  71.9 1.2 pad.91
  73.1 1.1 add.259
  74.2 1.4 convolution_bitcast_fusion.3
  75.7 1.0 pad_maximum_fusion.1
  76.7 2.2 pad.92
  78.9 3.0 %pad.93 = f32[1,8,256,256]{3,2,1,0:T(8,128)} pad(f32[1,4,256,256]{3,2,1,0:T(8,128)S(1)} %copy-done.8, f32[]{:T(128)} %constant.88.clone.1), padding=0_0_0x1_0_1x0_0_0x0_0_0 | pad | bytes 3145732 | tf_op jit(solution)/shard_map/pad | solution.py:60
  81.9 3.3 %add.260 = f32[1,8,256,256]{3,2,1,0:T(8,128)} add(f32[1,8,256,256]{3,2,1,0:T(8,128)S(1)} %pad.92, f32[1,8,256,256]{3,2,1,0:T(8,128)} %pad.93) | non-fusion elementwise | flops 524288 | bytes 6291456 | tf_op jit(solution)/shard_map/add | solution.py:60
  85.2 3.1 %rev.12 = f32[1,8,256,256]{3,2,1,0:T(8,128)} reverse(f32[1,8,256,256]{3,2,1,0:T(8,128)} %add.260), dimensions={1} | reverse | bytes 4194304 | tf_op jit(solution)/shard_map/jit(_flip)/rev | solution.py:63
  88.3 7.4 %all_gather.13 = f32[4,1,256]{2,1,0:T(1,128)S(1)} all-gather(f32[1,1,256]{2,1,0:T(1,128)S(1)} %slice_add_fusion.3), channel_id=1, replica_groups=mesh['grp'=2,'step'=4,'chain'=2,'rep'=2] {'step'}, dimensions={0}, use_global_device_ids=true | all-gather | bytes 5120 | tf_op jit(solution)/shard_map/all_gather | solution.py:15
  95.6 6.8 %all_gather.15 = f32[4,1,256]{2,1,0:T(1,128)S(1)} all-gather(f32[1,1,256]{2,1,0:T(1,128)S(1)} %slice_add_fusion.2), channel_id=1, replica_groups=mesh['grp'=2,'step'=4,'chain'=2,'rep'=2] {'step'}, dimensions={0}, use_global_device_ids=true | all-gather | bytes 5120 | tf_op jit(solution)/shard_map/all_gather | solution.py:15
  102.4 1.7 slice_add_fusion
  104.2 11.0 %while.33 = (s32[]{:T(128)}, f32[1,256,256]{2,1,0:T(8,128)S(1)}, f32[1,256]{1,0:T(1,128)S(1)}, s32[]{:T(128)}, f32[4,1,256,256]{3,2,1,0:T(8,128)}, /*index=5*/f32[4,1,256]{2,1,0:T(1,128)S(1)}, s32[]{:T(128)}, s32[]{:T(128)}) while((s32[]{:T(128)}, f32[1,256,256]{2,1,0:T(8,128)S(1)}, f32[1,256]{1,0:T(1,128)S(1)}, s32[]{:T(128)}, ...), condition=%wide.region_1.2_spmd.clone, body=%wide.region_0.1_spmd.clone.sunk | while | flops 202179584 | bytes 1845375 | solution.py:26
  104.3 1.3 fusion.138
  105.7 1.3 fusion.137
  107.1 1.2 fusion.138
  108.4 1.3 fusion.137
  109.8 1.2 fusion.138
  111.1 1.3 fusion.137
  112.5 1.2 fusion.138
  113.8 1.3 fusion.137
  115.2 1.0 fusion.28
  116.2 3.5 %fusion.19 = f32[1,8,256]{2,0,1:T(1,128)S(1)} fusion(f32[256,1,1]{0,1,2:T(1,128)S(1)} %fusion.28, f32[1,8,256,256]{3,2,1,0:T(8,128)S(1)} %copy-done.2, f32[1,8,256,256]{3,2,1,0:T(8,128)} %pad.81), kind=kOutput, calls=%fused_computation.27 | convolution fusion | flops 6815744 | bytes 4203520 | tf_op jit(solution)/shard_map/ctij,cj->cti/dot_general | solution.py:74
  119.8 14.8 %all-gather.5.cloned.1.call-done = f32[4,1,256,256]{3,2,1,0:T(8,128)} async-done(((f32[1,1,256,256]{3,2,1,0:T(8,128)}), f32[4,1,256,256]{3,2,1,0:T(8,128)}) %all-gather.5.cloned.1.call-update) | async-done | bytes 1048592 | tf_op jit(solution)/shard_map/all_gather | solution.py:15
  134.6 5.3 %while.34 = (s32[]{:T(128)}, f32[1,256]{1,0:T(1,128)S(1)}, s32[]{:T(128)}, f32[4,1,256,256]{3,2,1,0:T(8,128)}, f32[4,1,256]{2,1,0:T(1,128)S(1)}, /*index=5*/s32[]{:T(128)}, s32[]{:T(128)}, s32[]{:T(128)}, s32[]{:T(128)}) while((s32[]{:T(128)}, f32[1,256]{1,0:T(1,128)S(1)}, s32[]{:T(128)}, f32[4,1,256,256]{3,2,1,0:T(8,128)}, ...), condition=%wide.region_3.4_spmd.clone, body=%wide.region_2.3_spmd.clone.sunk | while | flops 787464 | bytes 272560 | solution.py:26
  134.6 1.2 fusion.141
  135.9 1.2 fusion.141
  137.3 1.2 fusion.141
  138.6 1.2 fusion.141
  139.9 3.4 %fusion.17 = f32[1,8,256]{2,0,1:T(1,128)S(1)} fusion(f32[1,8,256,256]{3,2,1,0:T(8,128)} %rev.12, f32[1,256]{1,0:T(1,128)S(1)} %get-tuple-element.247), kind=kOutput, calls=%fused_computation.25 | convolution fusion | flops 6291456 | bytes 2106368 | tf_op jit(solution)/shard_map/ctij,cj->cti/dot_general | solution.py:75
  143.4 30.3 %psum.15 = f32[256]{0:T(256)} all-reduce(f32[256]{0:T(256)S(1)} %broadcast_multiply_fusion), channel_id=1, replica_groups=mesh['grp'=2,'step'=4,'chain'=2,'rep'=2] {'step','chain','rep'}, use_global_device_ids=true, to_apply=%region_6.7 | all-reduce | flops 256 | bytes 2048 | tf_op jit(solution)/shard_map/psum | solution.py:81
  173.7 1.1 convolution_multiply_fusion
  175.5 88.6 %all-reduce.26.cloned.1.call-done = f32[256,256]{1,0:T(8,128)} async-done(((f32[256,256]{1,0:T(8,128)}), f32[256,256]{1,0:T(8,128)}) %all-reduce.26.cloned.1.call-update) | async-done | bytes 262160 | tf_op jit(solution)/shard_map/psum | solution.py:81
  264.1 1.7 copy.83
  (147 shorter events, 9.7 us)
Async XLA Ops:
  7.2 14.3 %copy-start.9 = (f32[256,256]{1,0:T(8,128)S(1)}, f32[256,256]{1,0:T(8,128)}, u32[]{:S(2)}) copy-start(f32[256,256]{1,0:T(8,128)} %param.17) | copy-start | bytes 786436
  7.2 97.0 %all-gather.3.cloned.1.call-start = ((), (), s32[]{:S(2)}) async-start(), calls=%async_computation | async-start | bytes 1310720 | tf_op jit(solution)/shard_map/all_gather | solution.py:15
  8.0 8.2 %collective-permute-start = (f32[1,256]{1,0:T(1,128)S(1)}, f32[1,256]{1,0:T(1,128)S(1)}, u32[]{:S(2)}, u32[]{:S(2)}) collective-permute-start(f32[1,256]{1,0:T(1,128)S(1)} %slice_bitcast_fusion.12), channel_id=1, source_target_pairs={{0,4},{4,8},{8,12},{1,5},{5,9},{9,13},{2,6},{6,10},{10,14},{3,7},{... | collective-permute-start | bytes 3080 | tf_op jit(solution)/shard_map/ppermute | solution.py:10
  24.2 9.1 %copy-start.12 = (f32[1,4,256]{2,1,0:T(4,128)}, f32[1,4,256]{2,1,0:T(4,128)S(1)}, u32[]{:S(2)}) copy-start(f32[1,4,256]{2,1,0:T(4,128)S(1)} %bitcast_add_fusion.3) | copy-start | bytes 12292
  24.2 2.8 %copy-start = (f32[1,8,256,256]{2,3,1,0:T(8,128)S(1)}, f32[1,8,256,256]{2,3,1,0:T(8,128)}, u32[]{:S(2)}) copy-start(f32[1,8,256,256]{2,3,1,0:T(8,128)} %get-tuple-element.324) | copy-start | bytes 6291460
  29.8 1.9 copy-start.3
  30.5 21.2 %copy-start.11 = (f32[1,4,256]{2,1,0:T(4,128)}, f32[1,4,256]{2,1,0:T(4,128)S(1)}, u32[]{:S(2)}) copy-start(f32[1,4,256]{2,1,0:T(4,128)S(1)} %bitcast_add_fusion.1) | copy-start | bytes 12292
  40.1 3.1 %copy-start.4 = (f32[1,4,256,256]{3,2,1,0:T(8,128)S(1)}, f32[1,4,256,256]{3,2,1,0:T(8,128)}, u32[]{:S(2)}) copy-start(f32[1,4,256,256]{3,2,1,0:T(8,128)} %pad.79) | copy-start | bytes 3145732
  50.0 4.3 %slice-start.1 = ((f32[1,4,256]{2,1,0:T(4,128)}), f32[1,1,256]{2,1,0:T(1,128)S(1)}, s32[]{:S(2)}) async-start(f32[1,4,256]{2,1,0:T(4,128)} %copy-done.12), calls=%async_computation.4 | async-start | bytes 2048 | tf_op jit(solution)/shard_map/slice | solution.py:57
  50.7 0.8 copy-start.6
  59.5 6.5 %copy-start.1 = (f32[1,8,256,256]{3,2,1,0:T(8,128)}, f32[1,8,256,256]{3,2,1,0:T(8,128)S(1)}, u32[]{:S(2)}) copy-start(f32[1,8,256,256]{3,2,1,0:T(8,128)S(1)} %pad.80) | copy-start | bytes 6291460
  59.6 6.5 %slice-start = ((f32[1,4,256]{2,1,0:T(4,128)}), f32[1,1,256]{2,1,0:T(1,128)S(1)}, s32[]{:S(2)}) async-start(f32[1,4,256]{2,1,0:T(4,128)} %copy-done.11), calls=%async_computation.3 | async-start | bytes 2048 | tf_op jit(solution)/shard_map/slice | solution.py:60
  66.0 68.6 %all-gather.5.cloned.1.call-start = ((), (), s32[]{:S(2)}) async-start(), calls=%async_computation.1 | async-start | bytes 1310720 | tf_op jit(solution)/shard_map/all_gather | solution.py:15
  66.1 2.8 %copy-start.7 = (f32[1,2,256,256]{3,2,1,0:T(8,128)S(1)}, f32[1,2,256,256]{3,2,1,0:T(8,128)}, u32[]{:S(2)}) copy-start(f32[1,2,256,256]{3,2,1,0:T(8,128)} %copy-done.6) | copy-start | bytes 1572868
  71.9 2.3 copy-start.5
  74.2 1.4 copy-start.10
  76.7 2.3 copy-start.8
  104.1 12.1 %copy-start.2 = (f32[1,8,256,256]{3,2,1,0:T(8,128)S(1)}, f32[1,8,256,256]{3,2,1,0:T(8,128)}, u32[]{:S(2)}) copy-start(f32[1,8,256,256]{3,2,1,0:T(8,128)} %copy-done.1) | copy-start | bytes 6291460
  104.2 159.9 %all-reduce.26.cloned.1.call-start = ((), (), s32[]{:S(2)}) async-start(), calls=%async_computation.2 | async-start | bytes 524288 | tf_op jit(solution)/shard_map/psum | solution.py:81
  119.7 23.6 %copy-start.14 = (f32[1,8,256]{2,1,0:T(8,128)S(1)}, f32[1,8,256]{2,1,0:T(8,128)}, u32[]{:S(2)}) copy-start(f32[1,8,256]{2,1,0:T(8,128)} %param.21) | copy-start | bytes 24580
  119.7 23.6 %copy-start.15 = (f32[256]{0:T(256)S(1)}, f32[256]{0:T(256)}, u32[]{:S(2)}) copy-start(f32[256]{0:T(256)} %param.18) | copy-start | bytes 3076
  119.7 54.0 %copy-start.13 = (f32[1,8,256]{2,1,0:T(8,128)S(1)}, f32[1,8,256]{2,1,0:T(8,128)}, u32[]{:S(2)}) copy-start(f32[1,8,256]{2,1,0:T(8,128)} %param.20) | copy-start | bytes 24580
Sparse Core Ops, SparseCore 0:
  66.1 28.3 all-gather.2
  104.3 30.2 all-gather.4
  175.0 89.0 all-reduce.25
where the time goes:
time: 274 us; the launch traced here: 272 us
  waiting for transfers between devices  104 us (38%)
  matrix products  46 us (17%)
  blocking collectives  44.4 us (16%)
  local copies, waits for them, and re-layouts  38.7 us (14%)
  other arithmetic  19.8 us (7%)
  between operations  15.1 us (6%)
  starting transfers between devices  4.14 us (2%)
    psum x1, waiting for transfers between devices, shards(): lax.psum((grad_local, bias_local), ('step', 'chain', 'rep'))  88.6 us
    psum x1, blocking collectives, shards(): lax.psum((grad_local, bias_local), ('step', 'chain', 'rep'))  30.3 us
    dot_general x14, matrix products, compose(): jnp.einsum('...ij,...jk->...ik', late_mat, early_mat, precision=highest)  17.2 us
    dot_general x18, matrix products, compose(): jnp.einsum('...ij,...j->...i', late_mat, early_vec, precision=highest)  16.1 us
    all_gather x2, waiting for transfers between devices, carried_in(): everything = jax.tree.map(lambda part: lax.all_gather(part, axis), x)  14.8 us
    all_gather x2, blocking collectives, carried_in(): everything = jax.tree.map(lambda part: lax.all_gather(part, axis), x)  14.2 us
    slice x18, local copies, waits for them, and re-layouts, shards(): lax.associative_scan(compose, (jnp.flip(transposed, 1), jnp.flip(source,...  11.3 us
    pad x8, local copies, waits for them, and re-layouts, shards(): lax.associative_scan(compose, (jacobian, offset), axis=1)  10.9 us
  transfers between devices with their start and end apart: 4, of which 2 were waited for; matrix products, arithmetic and copies ran while one was open for 16% of the time, Pallas kernels for 0%

commit v1 on v0

--- a/solution.py
+++ b/solution.py
@@ -2,6 +2,11 @@
 import jax.numpy as jnp
 from jax import lax
 from jax.sharding import PartitionSpec as P
+
+
+def one_after_other(value, one, other):
+    inner = lax.psum(value, one)
+    return lax.psum(inner, other)
 
 
 def shifted_2(block, axis, distance):
@@ -78,7 +83,7 @@
     weighted = adjoint * slope
     grad_local = step_size * jnp.einsum("cti,ctj->ij", weighted, previous, precision=highest)
     bias_local = step_size * jnp.sum(weighted, axis=(0, 1))
-    grad_w, grad_b = lax.psum((grad_local, bias_local), ("step", "chain", "rep"))
+    grad_w, grad_b = one_after_other((grad_local, bias_local), ("chain", "rep"), "step")
     return (path_new, grad_w, grad_b)
 
 

time: 274 us -> 225 us (0.82)
  waiting for transfers between devices: 104 us -> 65.1 us
  blocking collectives: 44.4 us -> 31.5 us
    psum x1 -> x2, waiting for transfers between devices: 88.6 us -> 45.4 us  [the longest x1 25.7 us: one_after_other(): inner = lax.psum(value, one)]
    psum x1 -> x2, blocking collectives: 30.3 us -> 17.4 us  [the longest x1 10.2 us: one_after_other(): return lax.psum(inner, other)]
    all_gather x2, waiting for transfers between devices: 14.8 us -> 19.6 us  [carried_in(): everything = jax.tree.map(lambda part: lax.all_gather(part, axis), x)]
  transfers between devices with their start and end apart: 4 -> 5, of which waited for: 2 -> 3; matrix products, arithmetic and copies ran while one was open for 16% -> 19% of each run, Pallas kernels for 0% -> 0%
where the time goes in v1:
time: 225 us; the launch traced here: 221 us
  waiting for transfers between devices  65.1 us (29%)
  matrix products  46 us (20%)
  local copies, waits for them, and re-layouts  38.7 us (17%)
  blocking collectives  31.5 us (14%)
  other arithmetic  19.8 us (9%)
  between operations  15.1 us (7%)
  starting transfers between devices  4.18 us (2%)
    psum x1, waiting for transfers between devices, one_after_other(): inner = lax.psum(value, one)  25.7 us
    psum x1, waiting for transfers between devices, one_after_other(): return lax.psum(inner, other)  19.8 us
    all_gather x2, waiting for transfers between devices, carried_in(): everything = jax.tree.map(lambda part: lax.all_gather(part, axis), x)  19.6 us
    dot_general x14, matrix products, compose(): jnp.einsum('...ij,...jk->...ik', late_mat, early_mat, precision=highest)  17.2 us
    dot_general x18, matrix products, compose(): jnp.einsum('...ij,...j->...i', late_mat, early_vec, precision=highest)  16.2 us
    all_gather x2, blocking collectives, carried_in(): everything = jax.tree.map(lambda part: lax.all_gather(part, axis), x)  14.1 us
    slice x18, local copies, waits for them, and re-layouts, shards(): lax.associative_scan(compose, (jnp.flip(transposed, 1), jnp.flip(source,...  11.3 us
    pad x8, local copies, waits for them, and re-layouts, shards(): lax.associative_scan(compose, (jacobian, offset), axis=1)  10.9 us
  transfers between devices with their start and end apart: 5, of which 3 were waited for; matrix products, arithmetic and copies ran while one was open for 19% of the time, Pallas kernels for 0%

profile of v1, /device:TPU:1, one launch (start us, length us, event | category | flops | bytes accessed | tf_op | source)
XLA Modules:
  0.0 221.0 jit_solution(8549606624488524329)
XLA Ops:
  8.0 4.0 %collective-permute-start = (f32[1,256]{1,0:T(1,128)S(1)}, f32[1,256]{1,0:T(1,128)S(1)}, u32[]{:S(2)}, u32[]{:S(2)}) collective-permute-start(f32[1,256]{1,0:T(1,128)S(1)} %slice_bitcast_fusion.12), channel_id=1, source_target_pairs={{0,4},{4,8},{8,12},{1,5},{5,9},{9,13},{2,6},{6,10},{10,14},{3,7},{... | collective-permute-start | bytes 3080 | tf_op jit(solution)/shard_map/ppermute | solution.py:15
  13.4 2.8 %gather_fusion = f32[8,256]{1,0:T(8,128)S(1)} fusion(f32[4096,256]{1,0:T(8,128)} %param.16, s32[1024]{0:T(1024)S(1)} %pad_clamp_fusion), kind=kCustom, calls=%fused_computation | custom fusion | bytes 16416 | tf_op jit(solution)/shard_map/gather | solution.py:56
  16.8 1.2 fusion.88
  18.1 0.8 multiply_bitcast_fusion
  18.9 2.4 %fusion.21 = f32[8,1,256]{2,1,0:T(1,128)S(1)} fusion(f32[256,256]{1,0:T(8,128)} %param.17, f32[8,256]{1,0:T(8,128)S(1)} %get-tuple-element.327, f32[256,256]{1,0:T(8,128)S(1)} %fusion.81, f32[8,256]{1,0:T(8,128)S(1)} %get-tuple-element.328, f32[8,256,1]{1,0,2:T(8,128)} %bitcast.301), kind=kOutput, calls=%fused_computation.29 | convolution fusion | flops 7864320 | bytes 557056 | tf_op jit(solution)/shard_map/ctij,ctj->cti/dot_general | solution.py:64
  21.5 1.7 fusion.83
  23.2 1.0 fusion.36
  24.9 2.1 slice.222
  27.0 1.5 fusion.121
  28.5 1.3 slice.225
  30.6 1.1 convolution_bitcast_fusion.2
  34.4 0.8 pad_add_fusion.1
  35.3 0.8 pad_maximum_fusion.2
  36.1 1.1 pad.78
  37.3 2.8 %pad.79 = f32[1,4,256,256]{3,2,1,0:T(8,128)} pad(f32[1,2,256,256]{3,2,1,0:T(8,128)} %pad_add_fusion.1, f32[]{:T(128)} %constant.88.clone.1), padding=0_0_0x1_0_1x0_0_0x0_0_0 | pad | bytes 1572868 | tf_op jit(solution)/shard_map/pad | solution.py:62
  40.0 3.1 %convolution_bitcast_fusion.4 = f32[1,3,256,256]{3,2,1,0:T(8,128)} fusion(f32[1,4,256,256]{3,2,1,0:T(8,128)} %pad.79, f32[1,4,256,256]{3,2,1,0:T(8,128)S(1)} %pad.78, f32[1,8,256,256]{3,2,1,0:T(8,128)S(1)} %get-tuple-element.325), kind=kOutput, calls=%fused_computation.38 | convolution fusion | flops 604176384 | bytes 3145728 | tf_op jit(solution)/shard_map/...ij,...jk->...ik/dot_general | solution.py:38
  43.1 1.1 add.250
  44.2 2.3 %slice.227 = f32[1,4,256,256]{2,3,1,0:T(8,128)} reverse(f32[1,4,256,256]{2,3,1,0:T(8,128)} %get-tuple-element.323), dimensions={1} | reverse | bytes 2097152 | tf_op jit(solution)/shard_map/slice | solution.py:65
  46.5 3.4 %convolution_bitcast_fusion.1 = f32[1,4,256,256]{3,2,1,0:T(8,128)S(1)} fusion(f32[1,4,256,256]{2,3,1,0:T(8,128)} %slice.227, f32[1,4,256,256]{2,3,1,0:T(8,128)} %copy-done.3), kind=kOutput, calls=%fused_computation.35 | convolution fusion | flops 805306368 | bytes 3145728 | tf_op jit(solution)/shard_map/...ij,...jk->...ik/dot_general | solution.py:38
  52.1 2.1 slice.223
  54.3 0.7 fusion.53
  55.0 2.3 %pad_maximum_fusion = f32[1,4,256,256]{3,2,1,0:T(8,128)} fusion(f32[1,3,256,256]{3,2,1,0:T(8,128)} %convolution_bitcast_fusion.4, f32[1,1,256,256]{3,2,1,0:T(8,128)} %slice.260), kind=kLoop, calls=%fused_computation.56 | loop fusion | flops 262144 | bytes 2097152 | tf_op jit(solution)/shard_map/concatenate | solution.py:62
  57.3 2.2 pad.80
  59.5 4.7 %pad.81 = f32[1,8,256,256]{3,2,1,0:T(8,128)} pad(f32[1,4,256,256]{3,2,1,0:T(8,128)} %add.250, f32[]{:T(128)} %constant.88.clone.1), padding=0_0_0x1_0_1x0_0_0x0_0_0 | pad | bytes 3145732 | tf_op jit(solution)/shard_map/pad | solution.py:62
  64.2 1.7 slice_add_fusion.1
  66.1 1.7 fusion.50
  67.8 1.0 slice.282
  68.9 0.9 copy.19
  71.0 0.9 pad_add_fusion
  71.9 1.2 pad.91
  73.1 1.1 add.263
  74.2 1.4 convolution_bitcast_fusion.3
  75.6 1.1 pad_maximum_fusion.1
  76.7 2.2 %pad.92 = f32[1,8,256,256]{3,2,1,0:T(8,128)S(1)} pad(f32[1,4,256,256]{3,2,1,0:T(8,128)} %pad_maximum_fusion.1, f32[]{:T(128)} %constant.88.clone.1), padding=0_0_0x0_1_1x0_0_0x0_0_0 | pad | bytes 3145732 | tf_op jit(solution)/shard_map/pad | solution.py:65
  79.0 3.0 %pad.93 = f32[1,8,256,256]{3,2,1,0:T(8,128)} pad(f32[1,4,256,256]{3,2,1,0:T(8,128)S(1)} %copy-done.8, f32[]{:T(128)} %constant.88.clone.1), padding=0_0_0x1_0_1x0_0_0x0_0_0 | pad | bytes 3145732 | tf_op jit(solution)/shard_map/pad | solution.py:65
  81.9 3.3 %add.264 = f32[1,8,256,256]{3,2,1,0:T(8,128)} add(f32[1,8,256,256]{3,2,1,0:T(8,128)S(1)} %pad.92, f32[1,8,256,256]{3,2,1,0:T(8,128)} %pad.93) | non-fusion elementwise | flops 524288 | bytes 6291456 | tf_op jit(solution)/shard_map/add | solution.py:65
  85.2 3.1 %rev.12 = f32[1,8,256,256]{3,2,1,0:T(8,128)} reverse(f32[1,8,256,256]{3,2,1,0:T(8,128)} %add.264), dimensions={1} | reverse | bytes 4194304 | tf_op jit(solution)/shard_map/jit(_flip)/rev | solution.py:68
  88.3 7.3 %all_gather.13 = f32[4,1,256]{2,1,0:T(1,128)S(1)} all-gather(f32[1,1,256]{2,1,0:T(1,128)S(1)} %slice_add_fusion.3), channel_id=1, replica_groups=mesh['grp'=2,'step'=4,'chain'=2,'rep'=2] {'step'}, dimensions={0}, use_global_device_ids=true | all-gather | bytes 5120 | tf_op jit(solution)/shard_map/all_gather | solution.py:20
  95.6 6.7 %all_gather.15 = f32[4,1,256]{2,1,0:T(1,128)S(1)} all-gather(f32[1,1,256]{2,1,0:T(1,128)S(1)} %slice_add_fusion.2), channel_id=1, replica_groups=mesh['grp'=2,'step'=4,'chain'=2,'rep'=2] {'step'}, dimensions={0}, use_global_device_ids=true | all-gather | bytes 5120 | tf_op jit(solution)/shard_map/all_gather | solution.py:20
  102.4 1.7 slice_add_fusion
  104.2 10.8 %while.33 = (s32[]{:T(128)}, f32[1,256,256]{2,1,0:T(8,128)S(1)}, f32[1,256]{1,0:T(1,128)S(1)}, s32[]{:T(128)}, f32[4,1,256,256]{3,2,1,0:T(8,128)}, /*index=5*/f32[4,1,256]{2,1,0:T(1,128)S(1)}, s32[]{:T(128)}, s32[]{:T(128)}) while((s32[]{:T(128)}, f32[1,256,256]{2,1,0:T(8,128)S(1)}, f32[1,256]{1,0:T(1,128)S(1)}, s32[]{:T(128)}, ...), condition=%wide.region_1.2_spmd.clone, body=%wide.region_0.1_spmd.clone.sunk | while | flops 202179584 | bytes 1845375 | solution.py:31
  104.2 1.2 fusion.138
  105.5 1.3 fusion.137
  106.9 1.2 fusion.138
  108.2 1.3 fusion.137
  109.6 1.2 fusion.138
  110.9 1.3 fusion.137
  112.3 1.2 fusion.138
  113.6 1.3 fusion.137
  115.0 19.6 %all-gather.5.cloned.1.call-done = f32[4,1,256,256]{3,2,1,0:T(8,128)} async-done(((f32[1,1,256,256]{3,2,1,0:T(8,128)}), f32[4,1,256,256]{3,2,1,0:T(8,128)}) %all-gather.5.cloned.1.call-update) | async-done | bytes 1048592 | tf_op jit(solution)/shard_map/all_gather | solution.py:20
  134.6 5.5 %while.34 = (s32[]{:T(128)}, f32[1,256]{1,0:T(1,128)S(1)}, s32[]{:T(128)}, f32[4,1,256,256]{3,2,1,0:T(8,128)}, f32[4,1,256]{2,1,0:T(1,128)S(1)}, /*index=5*/s32[]{:T(128)}, s32[]{:T(128)}, s32[]{:T(128)}, s32[]{:T(128)}) while((s32[]{:T(128)}, f32[1,256]{1,0:T(1,128)S(1)}, s32[]{:T(128)}, f32[4,1,256,256]{3,2,1,0:T(8,128)}, ...), condition=%wide.region_3.4_spmd.clone, body=%wide.region_2.3_spmd.clone.sunk | while | flops 787464 | bytes 272560 | solution.py:31
  134.6 1.4 fusion.141
  136.1 1.2 fusion.141
  137.4 1.2 fusion.141
  138.8 1.2 fusion.141
  140.1 3.4 %fusion.17 = f32[1,8,256]{2,0,1:T(1,128)S(1)} fusion(f32[1,8,256,256]{3,2,1,0:T(8,128)} %rev.12, f32[1,256]{1,0:T(1,128)S(1)} %get-tuple-element.247), kind=kOutput, calls=%fused_computation.25 | convolution fusion | flops 6291456 | bytes 2106368 | tf_op jit(solution)/shard_map/ctij,cj->cti/dot_general | solution.py:80
  143.6 1.1 convolution_multiply_fusion
  144.8 1.0 fusion.28
  145.9 3.5 %fusion.19 = f32[1,8,256]{2,0,1:T(1,128)S(1)} fusion(f32[256,1,1]{0,1,2:T(1,128)S(1)} %fusion.28, f32[1,8,256,256]{3,2,1,0:T(8,128)S(1)} %copy-done.2, f32[1,8,256,256]{3,2,1,0:T(8,128)} %pad.81), kind=kOutput, calls=%fused_computation.27 | convolution fusion | flops 6815744 | bytes 4203520 | tf_op jit(solution)/shard_map/ctij,cj->cti/dot_general | solution.py:79
  149.4 25.7 %all-reduce.27.cloned.1.call-done = f32[256,256]{1,0:T(8,128)} async-done(((f32[256,256]{1,0:T(8,128)}), f32[256,256]{1,0:T(8,128)}) %all-reduce.27.cloned.1.call-update) | async-done | bytes 262160 | tf_op jit(solution)/shard_map/psum | solution.py:8
  175.1 7.2 %psum.30 = f32[256]{0:T(256)S(1)} all-reduce(f32[256]{0:T(256)S(1)} %broadcast_multiply_fusion), channel_id=1, replica_groups=mesh['grp'=2,'step'=4,'chain'=2,'rep'=2] {'chain','rep'}, use_global_device_ids=true, to_apply=%region_7.8 | all-reduce | flops 256 | bytes 2048 | tf_op jit(solution)/shard_map/psum | solution.py:8
  182.3 10.2 %psum.31 = f32[256]{0:T(256)} all-reduce(f32[256]{0:T(256)S(1)} %psum.30), channel_id=1, replica_groups=mesh['grp'=2,'step'=4,'chain'=2,'rep'=2] {'step'}, use_global_device_ids=true, to_apply=%region_8.9 | all-reduce | flops 256 | bytes 2048 | tf_op jit(solution)/shard_map/psum | solution.py:9
  193.1 19.8 %all-reduce.29.cloned.1.call-done = f32[256,256]{1,0:T(8,128)} async-done(((f32[256,256]{1,0:T(8,128)}), f32[256,256]{1,0:T(8,128)}) %all-reduce.29.cloned.1.call-update) | async-done | bytes 262160 | tf_op jit(solution)/shard_map/psum | solution.py:9
  212.8 1.7 copy.84
  (151 shorter events, 11.2 us)
Async XLA Ops:
  7.2 14.3 %copy-start.9 = (f32[256,256]{1,0:T(8,128)S(1)}, f32[256,256]{1,0:T(8,128)}, u32[]{:S(2)}) copy-start(f32[256,256]{1,0:T(8,128)} %param.17) | copy-start | bytes 786436
  7.2 97.0 %all-gather.3.cloned.1.call-start = ((), (), s32[]{:S(2)}) async-start(), calls=%async_computation | async-start | bytes 1310720 | tf_op jit(solution)/shard_map/all_gather | solution.py:20
  8.0 8.2 %collective-permute-start = (f32[1,256]{1,0:T(1,128)S(1)}, f32[1,256]{1,0:T(1,128)S(1)}, u32[]{:S(2)}, u32[]{:S(2)}) collective-permute-start(f32[1,256]{1,0:T(1,128)S(1)} %slice_bitcast_fusion.12), channel_id=1, source_target_pairs={{0,4},{4,8},{8,12},{1,5},{5,9},{9,13},{2,6},{6,10},{10,14},{3,7},{... | collective-permute-start | bytes 3080 | tf_op jit(solution)/shard_map/ppermute | solution.py:15
  24.2 9.1 %copy-start.12 = (f32[1,4,256]{2,1,0:T(4,128)}, f32[1,4,256]{2,1,0:T(4,128)S(1)}, u32[]{:S(2)}) copy-start(f32[1,4,256]{2,1,0:T(4,128)S(1)} %bitcast_add_fusion.3) | copy-start | bytes 12292
  24.2 2.8 %copy-start = (f32[1,8,256,256]{2,3,1,0:T(8,128)S(1)}, f32[1,8,256,256]{2,3,1,0:T(8,128)}, u32[]{:S(2)}) copy-start(f32[1,8,256,256]{2,3,1,0:T(8,128)} %get-tuple-element.324) | copy-start | bytes 6291460
  29.8 1.9 copy-start.3
  30.5 21.2 %copy-start.11 = (f32[1,4,256]{2,1,0:T(4,128)}, f32[1,4,256]{2,1,0:T(4,128)S(1)}, u32[]{:S(2)}) copy-start(f32[1,4,256]{2,1,0:T(4,128)S(1)} %bitcast_add_fusion.1) | copy-start | bytes 12292
  40.0 3.1 %copy-start.4 = (f32[1,4,256,256]{3,2,1,0:T(8,128)S(1)}, f32[1,4,256,256]{3,2,1,0:T(8,128)}, u32[]{:S(2)}) copy-start(f32[1,4,256,256]{3,2,1,0:T(8,128)} %pad.79) | copy-start | bytes 3145732
  49.9 4.3 %slice-start.1 = ((f32[1,4,256]{2,1,0:T(4,128)}), f32[1,1,256]{2,1,0:T(1,128)S(1)}, s32[]{:S(2)}) async-start(f32[1,4,256]{2,1,0:T(4,128)} %copy-done.12), calls=%async_computation.5 | async-start | bytes 2048 | tf_op jit(solution)/shard_map/slice | solution.py:62
  50.6 0.8 copy-start.6
  59.5 6.5 %copy-start.1 = (f32[1,8,256,256]{3,2,1,0:T(8,128)}, f32[1,8,256,256]{3,2,1,0:T(8,128)S(1)}, u32[]{:S(2)}) copy-start(f32[1,8,256,256]{3,2,1,0:T(8,128)S(1)} %pad.80) | copy-start | bytes 6291460
  59.5 6.5 %slice-start = ((f32[1,4,256]{2,1,0:T(4,128)}), f32[1,1,256]{2,1,0:T(1,128)S(1)}, s32[]{:S(2)}) async-start(f32[1,4,256]{2,1,0:T(4,128)} %copy-done.11), calls=%async_computation.4 | async-start | bytes 2048 | tf_op jit(solution)/shard_map/slice | solution.py:65
  66.0 68.6 %all-gather.5.cloned.1.call-start = ((), (), s32[]{:S(2)}) async-start(), calls=%async_computation.1 | async-start | bytes 1310720 | tf_op jit(solution)/shard_map/all_gather | solution.py:20
  66.0 2.8 %copy-start.7 = (f32[1,2,256,256]{3,2,1,0:T(8,128)S(1)}, f32[1,2,256,256]{3,2,1,0:T(8,128)}, u32[]{:S(2)}) copy-start(f32[1,2,256,256]{3,2,1,0:T(8,128)} %copy-done.6) | copy-start | bytes 1572868
  71.9 2.3 %copy-start.5 = (f32[1,3,256,256]{2,3,1,0:T(8,128)S(1)}, f32[1,3,256,256]{2,3,1,0:T(8,128)}, u32[]{:S(2)}) copy-start(f32[1,3,256,256]{2,3,1,0:T(8,128)} %slice.223) | copy-start | bytes 2359300
  74.2 1.4 copy-start.10
  76.7 2.3 %copy-start.8 = (f32[1,4,256,256]{3,2,1,0:T(8,128)S(1)}, f32[1,4,256,256]{3,2,1,0:T(8,128)}, u32[]{:S(2)}) copy-start(f32[1,4,256,256]{3,2,1,0:T(8,128)} %add.263) | copy-start | bytes 3145732
  104.1 70.9 %all-reduce.27.cloned.1.call-start = ((), (), s32[]{:S(2)}) async-start(), calls=%async_computation.2 | async-start | bytes 524288 | tf_op jit(solution)/shard_map/psum | solution.py:8
  115.0 28.6 %copy-start.14 = (f32[1,8,256]{2,1,0:T(8,128)S(1)}, f32[1,8,256]{2,1,0:T(8,128)}, u32[]{:S(2)}) copy-start(f32[1,8,256]{2,1,0:T(8,128)} %param.21) | copy-start | bytes 24580
  115.0 28.5 %copy-start.15 = (f32[256]{0:T(256)S(1)}, f32[256]{0:T(256)}, u32[]{:S(2)}) copy-start(f32[256]{0:T(256)} %param.18) | copy-start | bytes 3076
  115.0 28.6 %copy-start.13 = (f32[1,8,256]{2,1,0:T(8,128)S(1)}, f32[1,8,256]{2,1,0:T(8,128)}, u32[]{:S(2)}) copy-start(f32[1,8,256]{2,1,0:T(8,128)} %param.20) | copy-start | bytes 24580
  134.6 11.2 %copy-start.2 = (f32[1,8,256,256]{3,2,1,0:T(8,128)S(1)}, f32[1,8,256,256]{3,2,1,0:T(8,128)}, u32[]{:S(2)}) copy-start(f32[1,8,256,256]{3,2,1,0:T(8,128)} %copy-done.1) | copy-start | bytes 6291460
  144.8 68.1 %all-reduce.29.cloned.1.call-start = ((), (), s32[]{:S(2)}) async-start(), calls=%async_computation.3 | async-start | bytes 524288 | tf_op jit(solution)/shard_map/psum | solution.py:9
Sparse Core Ops, SparseCore 0:
  66.1 28.3 all-gather.2
  104.2 30.3 all-gather.4
  144.9 30.0 all-reduce.26
  177.3 35.4 all-reduce.28
